TPU v7x, 32 devices: a whole 2x2x4 slice. The times are simulated.
32 devices in a mesh: kpt: 4 (over y, x), band: 8 (over z, core).
Axes of the slice: x: 2, y: 2, z: 4, core: 2. Of those that a mesh axis runs over, the one named last changes fastest.
Arguments:
- orbitals: bfloat16 [4, 8, 2, 48, 2304], P('kpt', 'band'), may hold values from -6 to 6
- kpoint_coords: int32 [4, 3], replicated, may hold values from 0 to 3, as said below
Outputs:
- exchange: bfloat16 [4, 8, 2, 48, 2304], P('kpt', 'band')
Inputs may be any that keep to these rules, and one draw needn't show every extreme that they name: `kpoint_coords`: the 4 rows are distinct points of the 4 x 4 x 4 grid.
All inputs are finite; a program needn't handle non-finite values.
Results may differ from a plain program's by a relative error of at most 0.0075.
The roundings to bfloat16 on the way count: a program that leaves them out, or rounds other values in their place, can miss the bound.
Values may be sent and summed in bfloat16 or wider, within the bound.
A program may use at most 64 MiB of HBM per device.

v0:
```python
import functools
import math

import jax
import jax.numpy as jnp
import ml_dtypes
import numpy as np
from jax import lax
from jax.experimental import pallas as pl
from jax.experimental.pallas import tpu as pltpu
from jax.sharding import PartitionSpec as P

SCREEN = 0.5
LANES = 128
GROUP = 4
PITCH_PAD = 8
MESH = pl.DeviceIdType.MESH


def dft_table(points, direction):
    indices = np.arange(points)
    angles = (indices[:, None] * indices[None, :] % points) * (2.0 * math.pi / points)
    scaling = 1.0 / math.sqrt(points)
    cosine = np.cos(angles) * scaling
    sine = direction * np.sin(angles) * scaling
    table = np.block([[cosine, -sine], [sine, cosine]])
    return table.astype(np.float32).astype(ml_dtypes.bfloat16)


def lane_table(points, direction):
    table = dft_table(points, direction).T
    wide = np.zeros((2 * LANES, 2 * LANES), table.dtype)
    for c in range(2):
        for d in range(2):
            block = table[c * points : (c + 1) * points, d * points : (d + 1) * points]
            for p in range(2):
                row, col = c * LANES + p * points, d * LANES + p * points
                wide[row : row + points, col : col + points] = block
    return wide


def dot(a, b):
    return jnp.dot(a, b, preferred_element_type=jnp.float32)


def side(blocks):
    return jnp.concatenate(blocks, axis=1)


def stack(blocks):
    return jnp.concatenate(blocks, axis=0)


def body(
    counts, points, coords, own, wf, wi, zf, zi, out,
    slots, own_wide, part_wide, grid_a, grid_b, total, send_sem, recv_sem,
):
    kpoints, bands = counts
    n = points
    pitch = 2 * n + PITCH_PAD
    bf16, f32 = jnp.bfloat16, jnp.float32
    k, b = lax.axis_index("kpt"), lax.axis_index("band")
    k_step = 1 - 2 * (k % 2)
    b_step = 1 - 2 * (b % 2)
    k_near = (k + k_step + kpoints) % kpoints
    k_far = (k - k_step + kpoints) % kpoints
    b_near = (b + b_step + bands) % bands
    b_far = (b - b_step + bands) % bands
    relay = kpoints == 4
    k_via = (k + 2) % kpoints if relay else k_far

    targets = [(k, b_near), (k_near, b), (k, b_far), (k_via, b)]
    barrier = pltpu.get_barrier_semaphore()
    for target in targets:
        pl.semaphore_signal(barrier, inc=1, device_id=target, device_id_type=MESH)
    pl.semaphore_wait(barrier, len(targets))

    def copy(i, source):
        return pltpu.make_async_remote_copy(
            src_ref=source, dst_ref=slots.at[i], send_sem=send_sem.at[i], recv_sem=recv_sem.at[i],
            device_id=targets[i], device_id_type=MESH,
        )

    copies = [copy(0, own), copy(1, own), copy(2, own), copy(3, slots.at[1] if relay else own)]
    copies[1].start()
    copies[2].start()
    copies[0].start()
    if not relay:
        copies[3].start()

    def widen(target, first, second):
        def chunk(h, carry):
            columns = pl.ds(pl.multiple_of(h * 8 * n, LANES), 8 * n)
            one = first[:, columns]
            two = one if second is first else (None if second is None else second[:, columns])
            blank = jnp.zeros((2 * n, LANES - 2 * n), bf16)
            gap = jnp.zeros((2 * n, n), bf16)
            for j in range(8):
                a = one[:, j * n : (j + 1) * n]
                c = gap if two is None else two[:, j * n : (j + 1) * n]
                target[h * 8 + j] = side([a, c, blank])
            return carry

        lax.fori_loop(0, n // 8, chunk, 0)

    lane = lax.broadcasted_iota(jnp.int32, (1, LANES), 1)
    upper = lane >= n
    z_at = jnp.where(upper, lane - n, lane)
    z_freq = jnp.where(z_at < n // 2, z_at, z_at - n).astype(f32)
    y_at = lax.broadcasted_iota(jnp.int32, (n, LANES), 0)
    y_freq = jnp.where(y_at < n // 2, y_at, y_at - n).astype(f32)
    cutoff = float((n // 2 - 1) ** 2)

    def offsets(first, second):
        def one(p, d):
            return (coords[k, d] - coords[p, d]).astype(f32) * 0.25

        return [jnp.where(upper, one(second, d), one(first, d)) for d in range(3)]

    def batch(first_k, second_k, is_first, between):
        q = offsets(first_k, second_k)
        yz = (y_freq + q[1]) ** 2 + (z_freq + q[2]) ** 2

        def phase_a(g, carry):
            fields = []
            for j in range(GROUP):
                y = g * GROUP + j
                o = own_wide[y].astype(f32)
                p = part_wide[y].astype(f32)
                o_re, o_im, p_re, p_im = o[:n], o[n:], p[:n], p[n:]
                fields.append(stack([p_re * o_re + p_im * o_im, p_re * o_im - p_im * o_re]).astype(bf16))
            r = dot(wf[...], side(fields))
            for j in range(GROUP):
                y = g * GROUP + j
                for c in range(2):
                    grid_a[pl.ds(c * n + y, n, stride=pitch), :] = r[c * n : (c + 1) * n, j * LANES : (j + 1) * LANES]
            return carry

        def planes(ref, g):
            return side(
                [ref[pl.ds(pl.multiple_of((g * GROUP + j) * pitch, 8), 2 * n), :].astype(bf16) for j in range(GROUP)]
            )

        def complex_rows(r):
            rows = []
            for j in range(GROUP):
                part = r[:, j * LANES : (j + 1) * LANES]
                rows.append(side([part[:n], part[n:]]))
            return stack(rows)

        def phase_b(g, carry):
            r = dot(wf[...], planes(grid_a, g)).astype(bf16)
            s = dot(complex_rows(r), zf[...])
            fields = []
            for j in range(GROUP):
                x = g * GROUP + j
                x_freq = jnp.where(x < n // 2, x, x - n).astype(f32)
                squared = (x_freq + q[0]) ** 2 + yz
                inside = (squared > 0.0) & (squared <= cutoff)
                kern = jnp.where(inside, 4.0 * math.pi / (squared + SCREEN), 0.0)
                part = s[j * n : (j + 1) * n]
                fields.append(stack([part[:, :LANES] * kern, part[:, LANES:] * kern]).astype(bf16))
            r = dot(wi[...], side(fields))
            for j in range(GROUP):
                x = g * GROUP + j
                for c in range(2):
                    grid_b[pl.ds(c * n + x, n, stride=pitch), :] = r[c * n : (c + 1) * n, j * LANES : (j + 1) * LANES]
            return carry

        def phase_c(g, carry):
            r = dot(wi[...], planes(grid_b, g)).astype(bf16)
            v = dot(complex_rows(r), zi[...]).astype(bf16).astype(f32)
            for j in range(GROUP):
                y = g * GROUP + j
                p = part_wide[y].astype(f32)
                v_re, v_im = v[j * n : (j + 1) * n, :LANES], v[j * n : (j + 1) * n, LANES:]
                term = stack([p[:n] * v_re - p[n:] * v_im, p[:n] * v_im + p[n:] * v_re])
                total[y] = term if is_first else total[y] + term
            return carry

        lax.fori_loop(0, n // GROUP, phase_a, 0)
        between()
        lax.fori_loop(0, n // GROUP, phase_b, 0)
        lax.fori_loop(0, n // GROUP, phase_c, 0)

    def start_relay():
        copies[1].wait_recv()
        if relay:
            copies[3].start()

    widen(own_wide, own, own)
    copies[0].wait_recv()
    widen(part_wide, own, slots.at[0])
    batch(k, k, True, start_relay)
    copies[2].wait_recv()
    widen(part_wide, slots.at[1], slots.at[2])
    batch(k_near, k, False, lambda: None)
    copies[3].wait_recv()
    widen(part_wide, slots.at[3], None)
    batch(k_far, k, False, lambda: None)

    def finish(h, carry):
        pieces = []
        for j in range(8):
            t = total[h * 8 + j]
            pieces.append(-(t[:, :n] + t[:, n : 2 * n]))
        out[:, pl.ds(pl.multiple_of(h * 8 * n, LANES), 8 * n)] = side(pieces).astype(bf16)
        return carry

    lax.fori_loop(0, n // 8, finish, 0)
    for c in copies:
        c.wait_send()


def on_device(counts, orbitals, kpoint_coords):
    points = orbitals.shape[3]
    cells = orbitals.shape[4]
    n = points
    own = orbitals.reshape(2 * n, cells)
    pitch = 2 * n + PITCH_PAD
    vmem = pl.BlockSpec(memory_space=pltpu.VMEM)
    smem = pl.BlockSpec(memory_space=pltpu.SMEM)
    result = pl.pallas_call(
        functools.partial(body, counts, points),
        out_shape=jax.ShapeDtypeStruct((2 * n, cells), jnp.bfloat16),
        in_specs=[smem] + [vmem] * 5,
        out_specs=vmem,
        scratch_shapes=[
            pltpu.VMEM((4, 2 * n, cells), jnp.bfloat16),
            pltpu.VMEM((n, 2 * n, LANES), jnp.bfloat16),
            pltpu.VMEM((n, 2 * n, LANES), jnp.bfloat16),
            pltpu.VMEM((n * pitch, LANES), jnp.float32),
            pltpu.VMEM((n * pitch, LANES), jnp.float32),
            pltpu.VMEM((n, 2 * n, LANES), jnp.float32),
            pltpu.SemaphoreType.DMA((4,)),
            pltpu.SemaphoreType.DMA((4,)),
        ],
        compiler_params=pltpu.CompilerParams(
            collective_id=0, has_side_effects=True, vmem_limit_bytes=40 * 1024 * 1024
        ),
    )(
        kpoint_coords, own,
        jnp.asarray(dft_table(n, -1.0)), jnp.asarray(dft_table(n, 1.0)),
        jnp.asarray(lane_table(n, -1.0)), jnp.asarray(lane_table(n, 1.0)),
    )
    return result.reshape(orbitals.shape)


def solution(mesh):
    counts = (mesh.shape["kpt"], mesh.shape["band"])
    return jax.shard_map(
        functools.partial(on_device, counts),
        mesh=mesh,
        in_specs=(P("kpt", "band", None, None, None), P()),
        out_specs=P("kpt", "band", None, None, None),
        check_vma=False,
    )
```

profile of v0, /device:TPU:0, one launch (start us, length us, event | category | flops | bytes accessed | tf_op | source)
XLA Modules:
  0.0 57.6 jit_solution(4069164564004931112)
XLA Ops:
  0.0 0.0 copy-start
  0.0 1.0 %copy-done = bf16[1,1,2,48,2304]{4,3,2,1,0:T(8,128)(2,1)S(1)} copy-done((bf16[1,1,2,48,2304]{4,3,2,1,0:T(8,128)(2,1)S(1)}, bf16[1,1,2,48,2304]{4,3,2,1,0:T(8,128)(2,1)}, u32[]{:S(2)}) %copy-start) | copy-done | bytes 442392
  1.0 0.0 copy-start.1
  1.0 0.9 %copy-done.1 = bf16[256,256]{1,0:T(8,128)(2,1)S(1)} copy-done((bf16[256,256]{1,0:T(8,128)(2,1)S(1)}, bf16[256,256]{1,0:T(8,128)(2,1)}, u32[]{:S(2)}) %copy-start.1) | copy-done | bytes 131096
  1.9 0.0 copy-start.2
  1.9 0.9 %copy-done.2 = bf16[256,256]{1,0:T(8,128)(2,1)S(1)} copy-done((bf16[256,256]{1,0:T(8,128)(2,1)S(1)}, bf16[256,256]{1,0:T(8,128)(2,1)}, u32[]{:S(2)}) %copy-start.2) | copy-done | bytes 131096
  2.8 0.0 copy-start.3
  2.8 0.7 %copy-done.3 = bf16[96,96]{1,0:T(8,128)(2,1)S(1)} copy-done((bf16[96,96]{1,0:T(8,128)(2,1)S(1)}, bf16[96,96]{1,0:T(8,128)(2,1)}, u32[]{:S(2)}) %copy-start.3) | copy-done | bytes 18456
  3.6 0.0 copy-start.4
  3.6 0.7 %copy-done.4 = bf16[96,96]{1,0:T(8,128)(2,1)S(1)} copy-done((bf16[96,96]{1,0:T(8,128)(2,1)S(1)}, bf16[96,96]{1,0:T(8,128)(2,1)}, u32[]{:S(2)}) %copy-start.4) | copy-done | bytes 18456
  4.3 0.0 copy-start.5
  4.3 0.7 %copy-done.5 = s32[4,3]{1,0:T(4,128)S(1)} copy-done((s32[4,3]{1,0:T(4,128)S(1)}, s32[4,3]{1,0:T(4,128)}, u32[]{:S(2)}) %copy-start.5) | copy-done | bytes 72
  5.0 51.9 %shard_map.64 = bf16[96,2304]{1,0:T(8,128)(2,1)S(1)} custom-call(s32[4,3]{1,0:T(4,128)S(1)} %copy-done.5, bf16[96,2304]{1,0:T(8,128)(2,1)S(1)} %bitcast.3, bf16[96,96]{1,0:T(8,128)(2,1)S(1)} %copy-done.4, bf16[96,96]{1,0:T(8,128)(2,1)S(1)} %copy-done.3, bf16[256,256]{1,0:T(8,128)(2,1)S(1)} %copy-done.2, bf16[256,256]{1,0:T(8,128)(2,1)S(1)} %copy-done.1), custom_call_target="tpu_custom_call" | custom-call | tf_op jit(solution)/shard_map/pallas_call | solution.py:223
  56.9 0.8 %copy.8 = bf16[1,1,2,48,2304]{4,3,2,1,0:T(8,128)(2,1)} copy(bf16[1,1,2,48,2304]{4,3,2,1,0:T(8,128)(2,1)S(1)} %bitcast.2) | data formatting | bytes 884736
Async XLA Ops:
  0.0 1.0 %copy-start = (bf16[1,1,2,48,2304]{4,3,2,1,0:T(8,128)(2,1)S(1)}, bf16[1,1,2,48,2304]{4,3,2,1,0:T(8,128)(2,1)}, u32[]{:S(2)}) copy-start(bf16[1,1,2,48,2304]{4,3,2,1,0:T(8,128)(2,1)} %param.6) | copy-start | bytes 1327108
  1.0 0.9 %copy-start.1 = (bf16[256,256]{1,0:T(8,128)(2,1)S(1)}, bf16[256,256]{1,0:T(8,128)(2,1)}, u32[]{:S(2)}) copy-start(bf16[256,256]{1,0:T(8,128)(2,1)} %constant.11.clone.zi) | copy-start | bytes 393220
  1.9 0.9 %copy-start.2 = (bf16[256,256]{1,0:T(8,128)(2,1)S(1)}, bf16[256,256]{1,0:T(8,128)(2,1)}, u32[]{:S(2)}) copy-start(bf16[256,256]{1,0:T(8,128)(2,1)} %constant.10.clone.zf) | copy-start | bytes 393220
  2.8 0.7 %copy-start.3 = (bf16[96,96]{1,0:T(8,128)(2,1)S(1)}, bf16[96,96]{1,0:T(8,128)(2,1)}, u32[]{:S(2)}) copy-start(bf16[96,96]{1,0:T(8,128)(2,1)} %constant.9.clone.wi) | copy-start | bytes 55300
  3.6 0.7 %copy-start.4 = (bf16[96,96]{1,0:T(8,128)(2,1)S(1)}, bf16[96,96]{1,0:T(8,128)(2,1)}, u32[]{:S(2)}) copy-start(bf16[96,96]{1,0:T(8,128)(2,1)} %constant.8.clone.wf) | copy-start | bytes 55300
  4.3 0.7 %copy-start.5 = (s32[4,3]{1,0:T(4,128)S(1)}, s32[4,3]{1,0:T(4,128)}, u32[]{:S(2)}) copy-start(s32[4,3]{1,0:T(4,128)} %coords.1) | copy-start | bytes 148
where the time goes:
time: 58 us; the launch traced here: 57.6 us
  Pallas kernels  51.9 us (89%)
  local copies, waits for them, and re-layouts  5.74 us (10%)
    pallas_call x1, Pallas kernels, on_device(): pl.pallas_call(functools.partial(body, counts, points), out_shape=jax.Sha...  51.9 us
    unnamed x13, local copies, waits for them, and re-layouts  5.74 us

commit v1 on v0

--- a/solution.py
+++ b/solution.py
@@ -12,7 +12,8 @@
 
 SCREEN = 0.5
 LANES = 128
-GROUP = 4
+GROUP = 24
+SLAB = 8
 PITCH_PAD = 8
 MESH = pl.DeviceIdType.MESH
 
@@ -52,8 +53,8 @@
 
 
 def body(
-    counts, points, coords, own, wf, wi, zf, zi, out,
-    slots, own_wide, part_wide, grid_a, grid_b, total, send_sem, recv_sem,
+    counts, points, coords_in, own_in, tables_in, out,
+    coords, own, tables, local_sem, slots, own_wide, part_wide, grid_a, grid_b, total, send_sem, recv_sem,
 ):
     kpoints, bands = counts
     n = points
@@ -70,38 +71,71 @@
     k_via = (k + 2) % kpoints if relay else k_far
 
     targets = [(k, b_near), (k_near, b), (k, b_far), (k_via, b)]
+    loads = [
+        pltpu.make_async_copy(source, target, local_sem.at[i])
+        for i, (source, target) in enumerate(((own_in, own), (tables_in, tables), (coords_in, coords)))
+    ]
+    for load in loads:
+        load.start()
+    wide = 2 * LANES
+    zf, zi = tables.at[:wide], tables.at[wide : 2 * wide]
+    wf = tables.at[2 * wide : 2 * wide + 2 * n, : 2 * n]
+    wi = tables.at[2 * wide + 2 * n :, : 2 * n]
+
     barrier = pltpu.get_barrier_semaphore()
     for target in targets:
         pl.semaphore_signal(barrier, inc=1, device_id=target, device_id_type=MESH)
     pl.semaphore_wait(barrier, len(targets))
 
-    def copy(i, source):
+    parts = n // SLAB
+
+    def slab(p):
+        return pl.ds(pl.multiple_of(p * SLAB * n, LANES), SLAB * n)
+
+    def copy(i, p):
+        source = slots.at[1] if relay and i == 3 else own_in
         return pltpu.make_async_remote_copy(
-            src_ref=source, dst_ref=slots.at[i], send_sem=send_sem.at[i], recv_sem=recv_sem.at[i],
+            src_ref=source.at[:, slab(p)], dst_ref=slots.at[i, :, slab(p)],
+            send_sem=send_sem.at[i, p], recv_sem=recv_sem.at[i, p],
             device_id=targets[i], device_id_type=MESH,
         )
 
-    copies = [copy(0, own), copy(1, own), copy(2, own), copy(3, slots.at[1] if relay else own)]
-    copies[1].start()
-    copies[2].start()
-    copies[0].start()
-    if not relay:
-        copies[3].start()
-
-    def widen(target, first, second):
-        def chunk(h, carry):
-            columns = pl.ds(pl.multiple_of(h * 8 * n, LANES), 8 * n)
-            one = first[:, columns]
-            two = one if second is first else (None if second is None else second[:, columns])
-            blank = jnp.zeros((2 * n, LANES - 2 * n), bf16)
-            gap = jnp.zeros((2 * n, n), bf16)
-            for j in range(8):
-                a = one[:, j * n : (j + 1) * n]
-                c = gap if two is None else two[:, j * n : (j + 1) * n]
-                target[h * 8 + j] = side([a, c, blank])
+    def each_part(step):
+        def run(p, carry):
+            step(p)
             return carry
 
-        lax.fori_loop(0, n // 8, chunk, 0)
+        lax.fori_loop(0, parts, run, 0)
+
+    def send_near(p):
+        copy(0, p).start()
+
+    def send_own(p):
+        copy(1, p).start()
+        copy(2, p).start()
+        if not relay:
+            copy(3, p).start()
+
+    each_part(send_near)
+    each_part(send_own)
+    for load in loads:
+        load.wait()
+
+    def pass_on(p):
+        copy(1, p).wait_recv()
+        if relay:
+            copy(3, p).start()
+
+    blank = jnp.zeros((2 * n, LANES - 2 * n), bf16)
+    gap = jnp.zeros((2 * n, n), bf16)
+
+    def widen(target, first, second, p):
+        one = first[:, slab(p)]
+        two = one if second is first else (None if second is None else second[:, slab(p)])
+        for j in range(SLAB):
+            a = one[:, j * n : (j + 1) * n]
+            c = gap if two is None else two[:, j * n : (j + 1) * n]
+            target[p * SLAB + j] = side([a, c, blank])
 
     lane = lax.broadcasted_iota(jnp.int32, (1, LANES), 1)
     upper = lane >= n
@@ -117,24 +151,27 @@
 
         return [jnp.where(upper, one(second, d), one(first, d)) for d in range(3)]
 
-    def batch(first_k, second_k, is_first, between):
+    def batch(first_k, second_k, is_first, first, second, before, between):
         q = offsets(first_k, second_k)
         yz = (y_freq + q[1]) ** 2 + (z_freq + q[2]) ** 2
 
-        def phase_a(g, carry):
+        def phase_a(g):
+            before(g)
+            if is_first:
+                widen(own_wide, own, own, g)
+            widen(part_wide, first, second, g)
             fields = []
-            for j in range(GROUP):
-                y = g * GROUP + j
+            for j in range(SLAB):
+                y = g * SLAB + j
                 o = own_wide[y].astype(f32)
                 p = part_wide[y].astype(f32)
                 o_re, o_im, p_re, p_im = o[:n], o[n:], p[:n], p[n:]
                 fields.append(stack([p_re * o_re + p_im * o_im, p_re * o_im - p_im * o_re]).astype(bf16))
             r = dot(wf[...], side(fields))
-            for j in range(GROUP):
-                y = g * GROUP + j
+            for j in range(SLAB):
+                y = g * SLAB + j
                 for c in range(2):
                     grid_a[pl.ds(c * n + y, n, stride=pitch), :] = r[c * n : (c + 1) * n, j * LANES : (j + 1) * LANES]
-            return carry
 
         def planes(ref, g):
             return side(
@@ -178,26 +215,22 @@
                 total[y] = term if is_first else total[y] + term
             return carry
 
-        lax.fori_loop(0, n // GROUP, phase_a, 0)
-        between()
+        each_part(phase_a)
+        between(0)
         lax.fori_loop(0, n // GROUP, phase_b, 0)
+        between(1)
         lax.fori_loop(0, n // GROUP, phase_c, 0)
 
-    def start_relay():
-        copies[1].wait_recv()
-        if relay:
-            copies[3].start()
-
-    widen(own_wide, own, own)
-    copies[0].wait_recv()
-    widen(part_wide, own, slots.at[0])
-    batch(k, k, True, start_relay)
-    copies[2].wait_recv()
-    widen(part_wide, slots.at[1], slots.at[2])
-    batch(k_near, k, False, lambda: None)
-    copies[3].wait_recv()
-    widen(part_wide, slots.at[3], None)
-    batch(k_far, k, False, lambda: None)
+    def before_second(p):
+        @pl.when(p >= 2)
+        def _():
+            pass_on(p)
+
+        copy(2, p).wait_recv()
+
+    batch(k, k, True, own, slots.at[0], lambda p: copy(0, p).wait_recv(), pass_on)
+    batch(k_near, k, False, slots.at[1], slots.at[2], before_second, lambda i: None)
+    batch(k_far, k, False, slots.at[3], None, lambda p: copy(3, p).wait_recv(), lambda i: None)
 
     def finish(h, carry):
         pieces = []
@@ -208,8 +241,12 @@
         return carry
 
     lax.fori_loop(0, n // 8, finish, 0)
-    for c in copies:
-        c.wait_send()
+
+    def drain(p):
+        for i in range(4):
+            copy(i, p).wait_send()
+
+    each_part(drain)
 
 
 def on_device(counts, orbitals, kpoint_coords):
@@ -218,30 +255,34 @@
     n = points
     own = orbitals.reshape(2 * n, cells)
     pitch = 2 * n + PITCH_PAD
-    vmem = pl.BlockSpec(memory_space=pltpu.VMEM)
-    smem = pl.BlockSpec(memory_space=pltpu.SMEM)
+    tables = np.zeros((4 * LANES + 4 * n, 2 * LANES), ml_dtypes.bfloat16)
+    for i, direction in enumerate((-1.0, 1.0)):
+        tables[2 * LANES * i : 2 * LANES * (i + 1)] = lane_table(n, direction)
+        tables[4 * LANES + 2 * n * i : 4 * LANES + 2 * n * (i + 1), : 2 * n] = dft_table(n, direction)
     result = pl.pallas_call(
         functools.partial(body, counts, points),
         out_shape=jax.ShapeDtypeStruct((2 * n, cells), jnp.bfloat16),
-        in_specs=[smem] + [vmem] * 5,
-        out_specs=vmem,
+        in_specs=[pl.BlockSpec(memory_space=pl.ANY)] * 3,
+        out_specs=pl.BlockSpec(memory_space=pltpu.VMEM),
         scratch_shapes=[
+            pltpu.SMEM(kpoint_coords.shape, jnp.int32),
+            pltpu.VMEM((2 * n, cells), jnp.bfloat16),
+            pltpu.VMEM(tables.shape, jnp.bfloat16),
+            pltpu.SemaphoreType.DMA((3,)),
             pltpu.VMEM((4, 2 * n, cells), jnp.bfloat16),
             pltpu.VMEM((n, 2 * n, LANES), jnp.bfloat16),
             pltpu.VMEM((n, 2 * n, LANES), jnp.bfloat16),
             pltpu.VMEM((n * pitch, LANES), jnp.float32),
             pltpu.VMEM((n * pitch, LANES), jnp.float32),
             pltpu.VMEM((n, 2 * n, LANES), jnp.float32),
-            pltpu.SemaphoreType.DMA((4,)),
-            pltpu.SemaphoreType.DMA((4,)),
+            pltpu.SemaphoreType.DMA((4, n // SLAB)),
+            pltpu.SemaphoreType.DMA((4, n // SLAB)),
         ],
         compiler_params=pltpu.CompilerParams(
-            collective_id=0, has_side_effects=True, vmem_limit_bytes=40 * 1024 * 1024
+            collective_id=0, has_side_effects=True, vmem_limit_bytes=60 * 1024 * 1024
         ),
     )(
-        kpoint_coords, own,
-        jnp.asarray(dft_table(n, -1.0)), jnp.asarray(dft_table(n, 1.0)),
-        jnp.asarray(lane_table(n, -1.0)), jnp.asarray(lane_table(n, 1.0)),
+        kpoint_coords, own, jnp.asarray(tables),
     )
     return result.reshape(orbitals.shape)
 

time: 58 us -> 28.8 us (0.50)
  Pallas kernels: 51.9 us -> 26.9 us
  local copies, waits for them, and re-layouts: 5.74 us -> 1.8 us
    pallas_call x1, Pallas kernels: 51.9 us -> 26.9 us  [on_device(): pl.pallas_call(functools.partial(body, counts, points), out_shape=jax.Sha...]
    unnamed x13 -> x1, local copies, waits for them, and re-layouts: 5.74 us -> 1.8 us
where the time goes in v1:
time: 28.8 us; the launch traced here: 28.7 us
  Pallas kernels  26.9 us (93%)
  local copies, waits for them, and re-layouts  1.8 us (6%)
    pallas_call x1, Pallas kernels, on_device(): pl.pallas_call(functools.partial(body, counts, points), out_shape=jax.Sha...  26.9 us
    unnamed x1, local copies, waits for them, and re-layouts  1.8 us

profile of v1, /device:TPU:0, one launch (start us, length us, event | category | flops | bytes accessed | tf_op | source)
XLA Modules:
  0.0 28.7 jit_solution(204561232640331251)
XLA Ops:
  0.0 26.9 %shard_map.37 = bf16[96,2304]{1,0:T(8,128)(2,1)} custom-call(s32[4,3]{1,0:T(4,128)} %coords_in.1, bf16[96,2304]{1,0:T(8,128)(2,1)} %bitcast.3, bf16[704,256]{1,0:T(8,128)(2,1)} %constant.2.clone.tables_in), custom_call_target="tpu_custom_call" | custom-call | tf_op jit(solution)/shard_map/pallas_call | solution.py:262
  26.9 1.8 %copy.5 = bf16[1,1,2,48,2304]{4,3,2,1,0:T(8,128)(2,1)} copy(bf16[1,1,2,48,2304]{4,3,2,1,0:T(8,128)(2,1)} %bitcast.2) | data formatting | bytes 884736
